TPU v7x, 256 devices: a whole 4x4x8 slice. The times are simulated.
256 devices in a mesh: region: 128 (over x, y, z), member: 2 (over core).
Axes of the slice: x: 4, y: 4, z: 8, core: 2. Of those that a mesh axis runs over, the one named last changes fastest.
Arguments:
- ensemble: float32 [983040, 256], P('region', 'member'), may hold values from -6 to 6
- couplings: bfloat16 [15360, 4, 64, 64], P('region'), may hold values from -0.375 to 0.375
- neighbours: int32 [15360, 4], P('region'), may hold values from 0 to 124, as said below
- destination: int32 [15360], P('region'), may hold values from 0 to 127, as said below
- obs_index: int32 [128, 512], P('region'), may hold values from 0 to 8191, as said below
- obs_class: int32 [128, 512], P('region'), may hold values from 0 to 4
- obs_error: float32 [128, 512], P('region'), may hold values from 0.5 to 2
- obs_value: float32 [128, 512], P('region'), may hold values from -8 to 8
Outputs:
- posterior_ensemble: bfloat16 [983040, 256], P('region', 'member')
Inputs may be any that keep to these rules, and one draw needn't show every extreme that they name: `neighbours`: entry 0 is the block itself (2 + i); entries 1 and 2 lie within 2 of it; entry 3 is within 2 of it or padding (124). Block 0 of every partition lists 0 and block 119 lists 120 + 2 * 2 - 1. `destination`: the blocks of one partition have distinct destinations, so at most 1 go from one partition to one region; some region receives a block in every one of its slots. `obs_index`: every observation reads a cell of a slot that holds a block.
All inputs are finite; a program needn't handle non-finite values.
Results may differ from a plain program's by a relative error of at most 0.0083.
Values may be sent and summed in bfloat16 or wider, within the bound.
A program may use at most 128 MiB of HBM per device.

v0:
```python
import jax
import jax.numpy as jnp
from jax import lax
from jax.sharding import PartitionSpec as P

HALO = 2
ITERS = 4


def padded(cells, sides, width):
    for axis, dim in sides:
        count = lax.axis_size(axis)
        ends = count - 1
        head = lax.slice_in_dim(cells, 0, width, axis=dim)
        tail = lax.slice_in_dim(cells, cells.shape[dim] - width, cells.shape[dim], axis=dim)
        cells = jnp.concatenate(
            [
                lax.ppermute(tail, axis, [(i, (i + 1) % count) for i in range(ends)]),
                cells,
                lax.ppermute(head, axis, [((i + 1) % count, i) for i in range(ends)]),
            ],
            axis=dim,
        )
    return cells


def newton(system):
    identity = jnp.eye(system.shape[0], dtype=jnp.float32)
    iterate = system
    inverse = identity
    for sweep in range(ITERS):
        update = 1.5 * identity - 0.5 * jnp.dot(inverse, iterate, precision=lax.Precision.HIGHEST)
        iterate = jnp.dot(iterate, update, precision=lax.Precision.HIGHEST)
        inverse = jnp.dot(update, inverse, precision=lax.Precision.HIGHEST)
    return inverse


def shards(
    ensemble, couplings, neighbours, destination, obs_index, obs_class, obs_error, obs_value
):
    block_count = neighbours.shape[0]
    own_members = ensemble.shape[1]
    cells_block = couplings.shape[2]
    member_states = own_members * lax.axis_size("member")
    regions = lax.axis_size("region")
    slots_peer = (block_count + regions - 1) // regions
    slot_count = regions * slots_peer
    field_now = ensemble.reshape(block_count, cells_block, own_members)
    for sweep in range(2):
        rounded = field_now.astype(jnp.bfloat16)
        extended = padded(rounded, (("region", 0),), HALO)
        extended = jnp.concatenate(
            [extended, jnp.zeros((1, cells_block, own_members), jnp.bfloat16)], axis=0
        )
        picked = extended[neighbours]
        field_now = jnp.einsum(
            "ijcd,ijdk->ick", couplings, picked, preferred_element_type=jnp.float32
        )
    outgoing = (
        jnp.zeros((slot_count, cells_block, own_members), jnp.bfloat16)
        .at[destination]
        .set(field_now.astype(jnp.bfloat16))
    )
    received = lax.all_to_all(outgoing, "region", split_axis=0, concat_axis=0, tiled=True)
    rows_per_slot = received.reshape(slot_count * cells_block, own_members)
    cell_mean = (
        lax.psum(jnp.sum(rows_per_slot, axis=1, dtype=jnp.float32), "member") / member_states
    )
    deviation = (rows_per_slot.astype(jnp.float32) - cell_mean[:, None]).astype(jnp.bfloat16)
    obs_rows = obs_index[0]
    local_pert = deviation[obs_rows].astype(jnp.float32)
    obs_pert = lax.all_gather(local_pert.astype(jnp.bfloat16), "member", axis=1, tiled=True).astype(
        local_pert.dtype
    )
    departure = obs_value[0] - cell_mean[obs_rows]
    weight = jnp.maximum(0.0, 1.0 - 0.25 * obs_class[0].astype(jnp.float32)) / obs_error[0]
    identity = jnp.eye(member_states, dtype=jnp.float32)
    gram_matrix = jnp.dot(obs_pert.T, obs_pert * weight[:, None], precision=lax.Precision.HIGHEST)
    system = (member_states - 1.0) * identity + gram_matrix
    frob_scale = jnp.sqrt(jnp.sum(system * system))
    root_inv = newton(system / frob_scale) / jnp.sqrt(frob_scale)
    innov_proj = jnp.dot(obs_pert.T, weight * departure, precision=lax.Precision.HIGHEST)
    mean_weights = jnp.dot(
        root_inv,
        jnp.dot(root_inv, innov_proj, precision=lax.Precision.HIGHEST),
        precision=lax.Precision.HIGHEST,
    )
    combined = (mean_weights[:, None] + jnp.sqrt(member_states - 1.0) * root_inv - identity).astype(
        jnp.bfloat16
    )
    first_member = lax.axis_index("member") * own_members
    own_rows = lax.dynamic_slice_in_dim(combined, first_member, own_members, 0)
    partial_term = jnp.dot(deviation, own_rows, preferred_element_type=jnp.float32)
    state_increment = lax.psum_scatter(partial_term, "member", scatter_dimension=1, tiled=True)
    incr_low = state_increment.astype(jnp.bfloat16)
    returned = lax.all_to_all(
        incr_low.reshape(regions, slots_peer * cells_block, own_members),
        "region",
        split_axis=0,
        concat_axis=0,
        tiled=True,
    )
    own_incr = returned[destination]
    posterior_ensemble = (field_now + own_incr.astype(jnp.float32)).astype(jnp.bfloat16)
    return posterior_ensemble.reshape(block_count * cells_block, own_members)


def solution(mesh):
    return jax.shard_map(
        shards,
        mesh=mesh,
        in_specs=(
            P("region", "member"),
            P("region", None, None, None),
            P("region", None),
            P("region"),
            P("region", None),
            P("region", None),
            P("region", None),
            P("region", None),
        ),
        out_specs=P("region", "member"),
        check_vma=False,
    )
```

profile of v0, /device:TPU:2, one launch (start us, length us, event | category | flops | bytes accessed | tf_op | source)
XLA Modules:
  0.0 298.5 jit_solution(487558232059183228)
XLA Ops:
  6.5 2.3 convert_element_type.57
  8.9 0.0 copy-start.1
  8.9 3.8 %collective-permute-start = (bf16[2,64,128]{2,1,0:T(8,128)(2,1)S(1)}, bf16[2,64,128]{2,1,0:T(8,128)(2,1)S(1)}, u32[]{:S(2)}, u32[]{:S(2)}) collective-permute-start(bf16[2,64,128]{2,1,0:T(8,128)(2,1)S(1)} %bitcast.76), channel_id=1, source_target_pairs={{0,2},{2,4},{4,6},{6,8},{8,10},{10,12},{12,14},{14,16},{16,18},{18... | collective-permute-start | bytes 98312 | tf_op jit(solution)/shard_map/ppermute | solution.py:18
  12.7 8.3 %collective-permute-start.1 = (bf16[2,64,128]{2,1,0:T(8,128)(2,1)S(1)}, bf16[2,64,128]{2,1,0:T(8,128)(2,1)S(1)}, u32[]{:S(2)}, u32[]{:S(2)}) collective-permute-start(bf16[2,64,128]{2,1,0:T(8,128)(2,1)S(1)} %bitcast.75), channel_id=1, source_target_pairs={{2,0},{4,2},{6,4},{8,6},{10,8},{12,10},{14,12},{16,14},{18,16},{20... | collective-permute-start | bytes 98312 | tf_op jit(solution)/shard_map/ppermute | solution.py:20
  21.0 0.0 copy-done.4
  21.0 0.1 copy.11
  21.1 0.1 reshape.70
  21.3 12.6 %copy.12 = bf16[120,4,64,64]{3,2,1,0:T(8,128)(2,1)} copy(bf16[120,4,64,64]{0,3,2,1:T(8,128)(2,1)} %param.9) | data formatting | bytes 7864320 | tf_op args[1]
  33.9 0.0 copy-done.1
  33.9 0.1 pad.7.clone
  34.0 0.0 collective-permute-done
  34.0 0.0 collective-permute-done.1
  34.0 1.9 maximum_maximum_fusion
  35.8 13.3 %gather_fusion = bf16[480,64,128]{2,1,0:T(8,128)(2,1)} fusion(bf16[125,64,128]{2,1,0:T(8,128)(2,1)S(1)} %maximum_maximum_fusion, s32[1024]{0:T(1024)S(1)} %pad_clamp_fusion.2), kind=kCustom, calls=%fused_computation | custom fusion | bytes 15730560 | tf_op jit(solution)/shard_map/gather | solution.py:55
  49.1 0.0 copy-start.7
  49.1 7.2 %fusion.2 = bf16[120,64,128]{2,1,0:T(8,128)(2,1)S(1)} fusion(bf16[120,4,64,64]{3,2,1,0:T(8,128)(2,1)} %copy.12, bf16[120,4,64,128]{3,2,1,0:T(8,128)(2,1)} %bitcast.73), kind=kOutput, calls=%fused_computation.14 | convolution fusion | flops 504299520 | bytes 13762560 | tf_op jit(solution)/shard_map/ijcd,ijdk->ick/dot_general | solution.py:56
  56.4 1.9 collective-permute-start.2
  58.3 8.3 %collective-permute-start.3 = (bf16[2,64,128]{2,1,0:T(8,128)(2,1)S(1)}, bf16[2,64,128]{2,1,0:T(8,128)(2,1)S(1)}, u32[]{:S(2)}, u32[]{:S(2)}) collective-permute-start(bf16[2,64,128]{2,1,0:T(8,128)(2,1)S(1)} %get-tuple-element.6), channel_id=1, source_target_pairs={{2,0},{4,2},{6,4},{8,6},{10,8},{12,10},{14,12},{16,14},{18,16},{20... | collective-permute-start | bytes 98312 | tf_op jit(solution)/shard_map/ppermute | solution.py:20
  66.6 0.0 copy-done.7
  66.7 0.0 collective-permute-done.2
  66.7 1.4 collective-permute-done.3
  68.0 0.3 maximum_maximum_fusion.1
  68.3 13.3 %gather_fusion.1 = bf16[480,64,128]{2,1,0:T(8,128)(2,1)} fusion(bf16[125,64,128]{2,1,0:T(8,128)(2,1)S(1)} %maximum_maximum_fusion.1, s32[1024]{0:T(1024)S(1)} %pad_clamp_fusion.2), kind=kCustom, calls=%fused_computation.1 | custom fusion | bytes 15730560 | tf_op jit(solution)/shard_map/gather | solution.py:55
  81.7 9.2 %bitcast_convert_fusion = (bf16[120,64,128]{2,1,0:T(8,128)(2,1)S(1)}, f32[120,128,64,1]{1,2,3,0:T(8,128)}) fusion(bf16[120,4,64,64]{3,2,1,0:T(8,128)(2,1)} %copy.12, bf16[120,4,64,128]{3,2,1,0:T(8,128)(2,1)} %bitcast.72), kind=kOutput, calls=%fused_computation.9 | convolution fusion | flops 504299520 | bytes 17694720 | tf_op jit(solution)/shard_map/ijcd,ijdk->ick/dot_general | solution.py:56
  90.8 1.9 broadcast_in_dim.7
  92.7 15.7 %scatter_fusion = bf16[128,64,128]{2,1,0:T(8,128)(2,1)} fusion(bf16[128,64,128]{2,1,0:T(8,128)(2,1)} %broadcast_in_dim.7, s32[120]{0:T(128)S(1)} %compare_select_fusion.2, bf16[120,64,128]{2,1,0:T(8,128)(2,1)S(1)} %get-tuple-element.9), kind=kCustom, calls=%fused_computation.5 | custom fusion | bytes 5898720 | tf_op jit(solution)/shard_map/scatter | solution.py:62
  108.4 12.5 %all-to-all-start = ((bf16[128,64,128]{2,1,0:T(8,128)(2,1)}), bf16[128,64,128]{2,1,0:T(8,128)(2,1)S(1)}, u32[]{:S(2)}, u32[]{:S(2)}) async-start(bf16[128,64,128]{2,1,0:T(8,128)(2,1)} %scatter_fusion), calls=%async_computation | async-start | bytes 4194304 | tf_op jit(solution)/shard_map/all_to_all | solution.py:64
  120.9 0.0 reduce-scatter.2.cloned.1.call-start
  121.0 0.0 copy-done.5
  121.0 0.0 copy-done.2
  121.1 50.0 %all-to-all-done = bf16[128,64,128]{2,1,0:T(8,128)(2,1)S(1)} async-done(((bf16[128,64,128]{2,1,0:T(8,128)(2,1)}), bf16[128,64,128]{2,1,0:T(8,128)(2,1)S(1)}, u32[]{:S(2)}, u32[]{:S(2)}) %all-to-all-start) | async-done | bytes 2097184 | tf_op jit(solution)/shard_map/all_to_all | solution.py:64
  171.0 1.2 convert_reduce_fusion
  172.2 0.1 reduce_sum.21
  172.3 3.6 %psum.7 = f32[8192]{0:T(1024)S(1)} all-reduce(f32[8192]{0:T(1024)S(1)} %reduce_sum.21), channel_id=1, replica_groups=mesh['region'=128,'member'=2] {'member'}, use_global_device_ids=true, to_apply=%region_2.0 | all-reduce | flops 8192 | bytes 65536 | tf_op jit(solution)/shard_map/psum | solution.py:67
  175.9 3.1 %gather_fusion.3 = f32[512]{0:T(512)S(1)} fusion(f32[8192]{0:T(1024)S(1)} %broadcast_multiply_fusion, s32[1024]{0:T(1024)S(1)} %pad_clamp_fusion.1), kind=kCustom, calls=%fused_computation.3 | custom fusion | bytes 6144 | tf_op jit(solution)/shard_map/gather | solution.py:75
  179.1 2.3 fusion
  181.3 2.9 gather_fusion.2
  184.2 2.0 all-gather
  186.2 1.1 multiply_reduce_fusion
  188.1 0.3 fusion.6
  188.4 0.4 fusion.15
  188.8 0.3 fusion.11
  189.1 0.4 fusion.5
  189.5 0.0 copy-start.6
  189.5 0.4 fusion.25
  189.9 0.4 fusion.24
  190.3 0.4 fusion.4
  190.7 0.4 fusion.27
  191.0 0.4 fusion.26
  191.5 0.2 convolution_bitcast_fusion.1
  191.7 0.4 fusion.3
  192.1 0.4 convolution_divide_fusion
  192.5 0.3 convolution_bitcast_fusion
  192.8 0.3 fusion.28
  193.1 0.1 dynamic-slice
  193.2 0.0 copy-done
  193.2 4.5 %fusion.16 = f32[8192,256]{1,0:T(8,128)} fusion(bf16[8192,128]{1,0:T(8,128)(2,1)S(1)} %copy-done, f32[256,256]{1,0:T(8,128)S(1)} %convolution_divide_fusion, s32[]{:T(128)S(6)} %select_n.25, pred[256,256]{1,0:T(32,128)(4,1)S(1)} %iota_compare_fusion, f32[128]{0:T(128)S(1)} %dynamic-slice), kind=kOutput, calls=%fused_computation.41 | convolution fusion | flops 537034752 | bytes 10650116 | tf_op jit(solution)/shard_map/dot_general | solution.py:93
  197.8 0.0 reduce-scatter.2.cloned.1.call-update
  197.8 17.2 %reduce-scatter.2.cloned.1.call-done = f32[8192,128]{1,0:T(8,128)} async-done(((f32[8192,256]{1,0:T(8,128)}), f32[8192,128]{1,0:T(8,128)}) %reduce-scatter.2.cloned.1.call-update) | async-done | bytes 4194320 | tf_op jit(solution)/shard_map/reduce_scatter | solution.py:94
  215.0 3.7 %convert_element_type.70 = bf16[8192,128]{1,0:T(8,128)(2,1)} convert(f32[8192,128]{1,0:T(8,128)} %reduce-scatter.2.cloned.1.call-done) | non-fusion elementwise | flops 1048576 | bytes 6291456 | tf_op jit(solution)/shard_map/convert_element_type | solution.py:95
  218.7 13.9 %all-to-all-start.1 = ((bf16[128,64,128]{2,1,0:T(8,128)(2,1)}), bf16[128,64,128]{2,1,0:T(8,128)(2,1)S(1)}, u32[]{:S(2)}, u32[]{:S(2)}) async-start(bf16[128,64,128]{2,1,0:T(8,128)(2,1)} %bitcast.24), calls=%async_computation.2 | async-start | bytes 4194304 | tf_op jit(solution)/shard_map/all_to_all | solution.py:96
  232.7 52.2 %all-to-all-done.1 = bf16[128,64,128]{2,1,0:T(8,128)(2,1)S(1)} async-done(((bf16[128,64,128]{2,1,0:T(8,128)(2,1)}), bf16[128,64,128]{2,1,0:T(8,128)(2,1)S(1)}, u32[]{:S(2)}, u32[]{:S(2)}) %all-to-all-start.1) | async-done | bytes 2097184 | tf_op jit(solution)/shard_map/all_to_all | solution.py:96
  284.9 2.1 gather_fusion.4
  287.0 4.7 %fusion.1 = bf16[120,64,128]{2,1,0:T(8,128)(2,1)} fusion(f32[120,128,64,1]{1,2,3,0:T(8,128)} %get-tuple-element.10, bf16[120,64,128]{2,1,0:T(8,128)(2,1)} %gather_fusion.4), kind=kLoop, calls=%fused_computation.10 | loop fusion | flops 2949120 | bytes 7864320 | tf_op jit(solution)/shard_map/convert_element_type | solution.py:104
  (19 shorter events, 0.1 us)
Async XLA Ops:
  6.5 14.5 %copy-start.4 = (s32[120,4]{0,1:T(4,128)S(1)}, s32[120,4]{0,1:T(4,128)}, u32[]{:S(2)}) copy-start(s32[120,4]{0,1:T(4,128)} %param.10) | copy-start | bytes 5764
  8.9 25.0 %copy-start.1 = (bf16[7680,128]{1,0:T(8,128)(2,1)}, bf16[7680,128]{1,0:T(8,128)(2,1)S(1)}, u32[]{:S(2)}) copy-start(bf16[7680,128]{1,0:T(8,128)(2,1)S(1)} %convert_element_type.57) | copy-start | bytes 5898244
  8.9 25.1 %collective-permute-start = (bf16[2,64,128]{2,1,0:T(8,128)(2,1)S(1)}, bf16[2,64,128]{2,1,0:T(8,128)(2,1)S(1)}, u32[]{:S(2)}, u32[]{:S(2)}) collective-permute-start(bf16[2,64,128]{2,1,0:T(8,128)(2,1)S(1)} %bitcast.76), channel_id=1, source_target_pairs={{0,2},{2,4},{4,6},{6,8},{8,10},{10,12},{12,14},{14,16},{16,18},{18... | collective-permute-start | bytes 98312 | tf_op jit(solution)/shard_map/ppermute | solution.py:18
  12.7 21.2 %collective-permute-start.1 = (bf16[2,64,128]{2,1,0:T(8,128)(2,1)S(1)}, bf16[2,64,128]{2,1,0:T(8,128)(2,1)S(1)}, u32[]{:S(2)}, u32[]{:S(2)}) collective-permute-start(bf16[2,64,128]{2,1,0:T(8,128)(2,1)S(1)} %bitcast.75), channel_id=1, source_target_pairs={{2,0},{4,2},{6,4},{8,6},{10,8},{12,10},{14,12},{16,14},{18,16},{20... | collective-permute-start | bytes 98312 | tf_op jit(solution)/shard_map/ppermute | solution.py:20
  49.1 17.5 %copy-start.7 = (s32[120]{0:T(128)S(1)}, s32[120]{0:T(128)}, u32[]{:S(2)}) copy-start(s32[120]{0:T(128)} %param.11) | copy-start | bytes 1444
  56.4 10.3 %collective-permute-start.2 = (bf16[2,64,128]{2,1,0:T(8,128)(2,1)S(1)}, bf16[2,64,128]{2,1,0:T(8,128)(2,1)S(1)}, u32[]{:S(2)}, u32[]{:S(2)}) collective-permute-start(bf16[2,64,128]{2,1,0:T(8,128)(2,1)S(1)} %get-tuple-element.5), channel_id=1, source_target_pairs={{0,2},{2,4},{4,6},{6,8},{8,10},{10,12},{12,14},{14,16},{16,18},{18... | collective-permute-start | bytes 98312 | tf_op jit(solution)/shard_map/ppermute | solution.py:18
  58.3 9.7 %collective-permute-start.3 = (bf16[2,64,128]{2,1,0:T(8,128)(2,1)S(1)}, bf16[2,64,128]{2,1,0:T(8,128)(2,1)S(1)}, u32[]{:S(2)}, u32[]{:S(2)}) collective-permute-start(bf16[2,64,128]{2,1,0:T(8,128)(2,1)S(1)} %get-tuple-element.6), channel_id=1, source_target_pairs={{2,0},{4,2},{6,4},{8,6},{10,8},{12,10},{14,12},{16,14},{18,16},{20... | collective-permute-start | bytes 98312 | tf_op jit(solution)/shard_map/ppermute | solution.py:20
  108.4 12.6 %copy-start.5 = (s32[1,512]{1,0:T(1,128)S(1)}, s32[1,512]{1,0:T(1,128)}, u32[]{:S(2)}) copy-start(s32[1,512]{1,0:T(1,128)} %param.12) | copy-start | bytes 6148
  108.4 12.6 %copy-start.2 = (f32[1,512]{1,0:T(1,128)S(1)}, f32[1,512]{1,0:T(1,128)}, u32[]{:S(2)}) copy-start(f32[1,512]{1,0:T(1,128)} %param.14) | copy-start | bytes 6148
  108.4 12.6 %copy-start.3 = (s32[1,512]{1,0:T(1,128)S(1)}, s32[1,512]{1,0:T(1,128)}, u32[]{:S(2)}) copy-start(s32[1,512]{1,0:T(1,128)} %param.13) | copy-start | bytes 6148
  108.4 62.6 %all-to-all-start = ((bf16[128,64,128]{2,1,0:T(8,128)(2,1)}), bf16[128,64,128]{2,1,0:T(8,128)(2,1)S(1)}, u32[]{:S(2)}, u32[]{:S(2)}) async-start(bf16[128,64,128]{2,1,0:T(8,128)(2,1)} %scatter_fusion), calls=%async_computation | async-start | bytes 4194304 | tf_op jit(solution)/shard_map/all_to_all | solution.py:64
  120.9 94.1 %reduce-scatter.2.cloned.1.call-start = ((), (), s32[]{:S(2)}) async-start(), calls=%async_computation.3 | async-start | bytes 12582912 | tf_op jit(solution)/shard_map/reduce_scatter | solution.py:94
  189.5 2.0 copy-start.6
  190.6 2.6 copy-start
  218.7 66.1 %all-to-all-start.1 = ((bf16[128,64,128]{2,1,0:T(8,128)(2,1)}), bf16[128,64,128]{2,1,0:T(8,128)(2,1)S(1)}, u32[]{:S(2)}, u32[]{:S(2)}) async-start(bf16[128,64,128]{2,1,0:T(8,128)(2,1)} %bitcast.24), calls=%async_computation.2 | async-start | bytes 4194304 | tf_op jit(solution)/shard_map/all_to_all | solution.py:96
Sparse Core Ops, SparseCore 0:
  197.9 17.0 reduce-scatter.1
where the time goes:
time: 302 us; the launch traced here: 298 us
  waiting for transfers between devices  121 us (40%)
  local copies, waits for them, and re-layouts  65.5 us (22%)
  starting transfers between devices  48.8 us (16%)
  matrix products  26.9 us (9%)
  other arithmetic  16.4 us (5%)
  between operations  14.5 us (5%)
  blocking collectives  5.61 us (2%)
    all_to_all x1, waiting for transfers between devices, shards(): lax.all_to_all(incr_low.reshape(regions, slots_peer * cells_block, own_me...  52.2 us
    all_to_all x1, waiting for transfers between devices, shards(): lax.all_to_all(outgoing, 'region', split_axis=0, concat_axis=0, tiled=True)  50 us
    gather x2, local copies, waits for them, and re-layouts, shards(): picked = extended[neighbours]  26.6 us
    reduce_scatter x1, waiting for transfers between devices, shards(): lax.psum_scatter(partial_term, 'member', scatter_dimension=1, tiled=True)  17.2 us
    ppermute x2, starting transfers between devices, padded(): lax.ppermute(head, axis, [((i + 1) % count, i) for i in range(ends)])  16.6 us
    dot_general x2, matrix products, shards(): jnp.einsum('ijcd,ijdk->ick', couplings, picked, preferred_element_type=jn...  16.4 us
    scatter x1, local copies, waits for them, and re-layouts, shards(): outgoing = jnp.zeros((slot_count, cells_block, own_members), jnp.bfloat16...  15.7 us
    all_to_all x1, starting transfers between devices, shards(): lax.all_to_all(incr_low.reshape(regions, slots_peer * cells_block, own_me...  13.9 us
  transfers between devices with their start and end apart: 7, of which 4 were waited for; matrix products, arithmetic and copies ran while one was open for 4% of the time, Pallas kernels for 0%

commit v1 on v0

v1 whole, which is shorter than its diff:
```python
import functools
import jax
import jax.numpy as jnp
from jax import lax
from jax.experimental import pallas as pl
from jax.experimental.pallas import tpu as pltpu
from jax.sharding import PartitionSpec as P

MESH = pl.DeviceIdType.MESH
NX, NY, NZ = 4, 4, 8
NQ = NX * NY
REGIONS = NQ * NZ
BLOCKS = 120
CELLS = 64
OWN = 128
MEMBERS = 256
OBS = 512
NEIGHB = 4
ITERS = 4
ROWS = NQ * CELLS
GROUP = 8
HALO = 2
WINDOW = 8
PART = OWN + 16
CHUNKS = ROWS // OWN
F32 = jnp.float32
BF16 = jnp.bfloat16
SHIFTS = sorted(
    [(a, b) for a in range(NX) for b in range(NY) if (a, b) != (0, 0)],
    key=lambda s: min(s[0], NX - s[0]) + min(s[1], NY - s[1]),
)


def depth_shift(k):
    return 4 + (1 - 2 * (k % 2)) * ((k + 1) // 2)


def bfdot(a, b):
    return jnp.dot(a, b, preferred_element_type=F32)


def halves(a):
    hi = a.astype(BF16)
    return hi, (a - hi.astype(F32)).astype(BF16)


def matmul(a, b):
    return bfdot(a[0], b[0]) + bfdot(a[0], b[1]) + bfdot(a[1], b[0])


def kernel(
    nbr, nbr_rows, dest, dest_row, ens_hbm, cpl_hbm, obs_index, obs_class, obs_error, obs_value, out,
    inv, inv_rows, ens, raw, turned_cpl, cmat, own0, low, high, ext1, cmat_far, nbr_send, nbr_recv, nbr_far, fc, send, recv, sib, po, ps, ret_send, ret_recv,
    vu_send, vu_recv, part_send, part_recv, mx_send, mx_recv, g_recv,
    ens_sem, cpl_sem, inv_sem, far_sem, halo_send, halo_recv, a_send, a_recv, sx_send, sx_recv,
    vu_ssem, vu_rsem, p_ssem, p_rsem, m_ssem, m_rsem, g_ssem, g_rsem, r_ssem, r_rsem,
):
    me = lax.axis_index("region")
    core = lax.axis_index("member")
    q_me = me // NZ
    z = me % NZ
    x = q_me // NY
    y = q_me % NY

    def plane_peer(dx, dy):
        return ((x + dx) % NX) * NY + (y + dy) % NY

    def remote(src, dst, ssem, rsem, region, member):
        return pltpu.make_async_remote_copy(
            src_ref=src, dst_ref=dst, send_sem=ssem, recv_sem=rsem,
            device_id=(region, member), device_id_type=MESH,
        )

    right = (me + 1) % REGIONS
    left = (me + REGIONS - 1) % REGIONS

    edges = [(0, GROUP), (BLOCKS - GROUP, GROUP), (GROUP, BLOCKS - 2 * GROUP)]
    ens_copies = [
        pltpu.make_async_copy(ens_hbm.at[pl.ds(a, n)], ens.at[pl.ds(a, n)], ens_sem.at[i])
        for i, (a, n) in enumerate(edges)
    ]
    for c in ens_copies[:2]:
        c.start()
    cpl_copies = [
        pltpu.make_async_copy(cpl_hbm.at[j], raw.at[j], cpl_sem.at[j]) for j in range(NEIGHB)
    ]
    for c in cpl_copies + ens_copies[2:]:
        c.start()

    barrier = pltpu.get_barrier_semaphore()
    peers = [(plane_peer(dx, dy) * NZ + z, core) for dx, dy in SHIFTS]
    peers += [(q_me * NZ + (z + d) % NZ, core) for d in range(1, NZ)]
    peers += [(me, 1 - core), (right, core), (left, core)]
    for p in peers:
        pl.semaphore_signal(barrier, 1, device_id=p, device_id_type=MESH)
    zero_block = jnp.zeros((1, CELLS, OWN), BF16)
    own0[pl.ds(BLOCKS, 1)] = zero_block
    low[pl.ds(WINDOW, 1)] = zero_block
    high[pl.ds(WINDOW, 1)] = zero_block
    ext1[pl.ds(BLOCKS + 4, 1)] = zero_block

    hit = lax.broadcasted_iota(jnp.int32, (REGIONS, BLOCKS), 0) == dest_row[...]
    numbers = (lax.broadcasted_iota(jnp.int32, (8, BLOCKS), 1) + 1).astype(F32).astype(BF16)
    found = lax.dot_general(
        numbers, jnp.where(hit, 1.0, 0.0).astype(BF16), (((1,), (1,)), ((), ())),
        preferred_element_type=F32,
    )
    inv_rows[...] = jnp.minimum(found, float(BLOCKS)).astype(jnp.int32) - 1
    inv_copy = pltpu.make_async_copy(inv_rows, inv, inv_sem)
    inv_copy.start()

    def cast(a, n):
        own0[pl.ds(a, n)] = ens[pl.ds(a, n)].astype(BF16)

    def to_sides(i, upper, lower, from_left, from_right):
        return [
            remote(upper, from_left, halo_send.at[2 * i], halo_recv.at[2 * i], right, core),
            remote(lower, from_right, halo_send.at[2 * i + 1], halo_recv.at[2 * i + 1], left, core),
        ]

    ens_copies[0].wait()
    cast(0, GROUP)
    ens_copies[1].wait()
    cast(BLOCKS - GROUP, GROUP)
    pl.semaphore_wait(barrier, len(peers))
    nbr_send[...] = jnp.zeros_like(nbr_send)
    nbr_send[0:NEIGHB, 0:BLOCKS] = nbr_rows[...]
    sides = to_sides(0, own0.at[pl.ds(BLOCKS - 4, 4)], own0.at[pl.ds(0, 4)],
                     low.at[pl.ds(0, 4)], high.at[pl.ds(4, 4)])
    lists = to_sides(1, nbr_send, nbr_send, nbr_recv.at[0], nbr_recv.at[1])
    for c in sides + lists:
        c.start()
    low[pl.ds(4, 4)] = own0[pl.ds(0, 4)]
    high[pl.ds(0, 4)] = own0[pl.ds(BLOCKS - 4, 4)]

    for pair in range(NEIGHB // 2):
        cpl_copies[2 * pair].wait()
        cpl_copies[2 * pair + 1].wait()

        @pl.loop(0, CELLS // GROUP)
        def _(g):
            for t in range(GROUP):
                c = g * GROUP + t
                slab = raw[pl.ds(2 * pair, 2), c].reshape(2 * CELLS, BLOCKS)
                turned_cpl[pair, pl.ds(pl.multiple_of(c * BLOCKS, 8), BLOCKS)] = slab.T.astype(F32)

    ens_copies[2].wait()

    @pl.loop(1, BLOCKS // GROUP - 1)
    def _(g):
        cast(g * GROUP, GROUP)


    def couple(i):
        cmat[i] = jnp.concatenate(
            [turned_cpl[pair, pl.ds(i, CELLS, stride=BLOCKS)] for pair in range(NEIGHB // 2)],
            axis=1,
        ).astype(BF16)

    def route(coeff, ext, places):
        return bfdot(coeff, jnp.concatenate([ext[p] for p in places], axis=0))

    for i in (0, 1, BLOCKS - 2, BLOCKS - 1):
        couple(i)
    coeffs = to_sides(2, cmat.at[pl.ds(BLOCKS - 2, 2)], cmat.at[pl.ds(0, 2)],
                      cmat_far.at[pl.ds(0, 2)], cmat_far.at[pl.ds(2, 2)])
    for c in coeffs:
        c.start()

    def inner(i):
        couple(i)
        places = [jnp.clip(nbr[j, i] - HALO, 0, BLOCKS) for j in range(NEIGHB)]
        ext1[i + HALO] = route(cmat[i], own0, places).astype(BF16)

    @pl.loop(0, (BLOCKS - 4) // GROUP)
    def _(g):
        for t in range(GROUP):
            inner(HALO + g * GROUP + t)

    for i in range(HALO + (BLOCKS - 4) // GROUP * GROUP, BLOCKS - HALO):
        inner(i)

    for c in lists:
        c.wait()
    far_copy = pltpu.make_async_copy(nbr_recv, nbr_far, far_sem)
    far_copy.start()
    for c in sides:
        c.wait()

    @pl.when(me == 0)
    def _():
        low[pl.ds(0, 4)] = jnp.zeros((4, CELLS, OWN), BF16)

    @pl.when(me == REGIONS - 1)
    def _():
        high[pl.ds(4, 4)] = jnp.zeros((4, CELLS, OWN), BF16)

    def first(e):
        return jnp.clip(e + 2, 0, WINDOW)

    def final(e):
        return jnp.clip(jnp.where(e == BLOCKS + 2 * HALO, WINDOW, e - (BLOCKS - 2)), 0, WINDOW)

    for t in range(HALO):
        i = BLOCKS - HALO + t
        places = [first(nbr[j, t]) for j in range(NEIGHB)]
        ext1[t + HALO] = route(cmat[t], low, places).astype(BF16)
        places = [final(nbr[j, i]) for j in range(NEIGHB)]
        ext1[i + HALO] = route(cmat[i], high, places).astype(BF16)
    for c in coeffs:
        c.wait()
    far_copy.wait()
    for t in range(HALO):
        i = BLOCKS - HALO + t
        places = [final(nbr_far[0, j, i]) for j in range(NEIGHB)]
        ext1[t] = route(cmat_far[t], low, places).astype(BF16)
        places = [first(nbr_far[1, j, t]) for j in range(NEIGHB)]
        ext1[BLOCKS + HALO + t] = route(cmat_far[HALO + t], high, places).astype(BF16)

    @pl.when(me == 0)
    def _():
        ext1[pl.ds(0, HALO)] = jnp.zeros((HALO, CELLS, OWN), BF16)

    @pl.when(me == REGIONS - 1)
    def _():
        ext1[pl.ds(BLOCKS + HALO, HALO)] = jnp.zeros((HALO, CELLS, OWN), BF16)

    inv_copy.wait()

    @pl.loop(0, NZ)
    def _(k):
        zr = (z + depth_shift(k)) % NZ
        for q in range(NQ):
            r = q * NZ + zr
            b = inv[0, r]
            held = jnp.clip(b, 0, BLOCKS - 1)
            field = route(cmat[held], ext1, [nbr[j, held] for j in range(NEIGHB)])
            field = jnp.where(b >= 0, field, 0.0)
            fc[r] = field
            send[k, q] = field.astype(BF16)
        recv[k, q_me] = send[k, q_me]
        for dx, dy in SHIFTS:
            to = plane_peer(dx, dy)
            remote(send.at[k, to], recv.at[k, q_me], a_send.at[k], a_recv.at[k],
                   to * NZ + z, core).start()

    index = obs_index[...]
    weight = jnp.maximum(0.0, 1.0 - 0.25 * obs_class[...].astype(F32)) / obs_error[...]
    value = weight * obs_value[...]
    place = (index // (CELLS * NZ)) * CELLS + index % CELLS
    plane = (index // CELLS) % NZ
    plane_hit = lax.broadcasted_iota(jnp.int32, (NZ, OBS), 0) == plane

    def three(a):
        hi = a.astype(BF16).astype(F32)
        mid = (a - hi).astype(BF16).astype(F32)
        low = a - hi - mid
        return [hi, mid, low]

    pieces = three(weight) + three(value)
    lhs = jnp.concatenate([jnp.where(plane_hit, p, 0.0) for p in pieces], axis=0).astype(BF16)
    cell_hit = jnp.where(
        lax.broadcasted_iota(jnp.int32, (ROWS, OBS), 0) == place, 1.0, 0.0
    ).astype(BF16)
    sums = lax.dot_general(lhs, cell_hit, (((1,), (1,)), ((), ())), preferred_element_type=F32)
    v_all = sums[0:NZ] + sums[NZ:2 * NZ] + sums[2 * NZ:3 * NZ]
    u_all = sums[3 * NZ:4 * NZ] + sums[4 * NZ:5 * NZ] + sums[5 * NZ:6 * NZ]
    for p in range(NZ):
        for c in range(CHUNKS):
            lanes = slice(c * OWN, (c + 1) * OWN)
            vu_send[p, c:c + 1] = v_all[p:p + 1, lanes]
            vu_send[p, CHUNKS + c:CHUNKS + c + 1] = u_all[p:p + 1, lanes]
    vu_recv[NZ - 1] = vu_send[z]

    @pl.loop(0, NZ - 1)
    def _(k):
        to = (z + NZ - depth_shift(k)) % NZ
        remote(vu_send.at[to], vu_recv.at[k], vu_ssem.at[k], vu_rsem.at[k],
               q_me * NZ + to, core).start()

    ones = jnp.ones((OWN, OWN), BF16)
    eye = (lax.broadcasted_iota(jnp.int32, (OWN, OWN), 0)
           == lax.broadcasted_iota(jnp.int32, (OWN, OWN), 1))

    def start_exchange(k):
        pltpu.make_async_copy(
            recv.at[k, pl.ds(0, NQ - 1)], recv.at[k, pl.ds(0, NQ - 1)], a_recv.at[k]
        ).wait()
        remote(recv.at[k], sib.at[k], sx_send.at[k], sx_recv.at[k], me, 1 - core).start()

    @pl.loop(0, NZ)
    def _(k):
        start_exchange(k)
        own = recv[k].reshape(ROWS, OWN)
        total = bfdot(own, ones)
        remote(recv.at[k], sib.at[k], sx_send.at[k], sx_recv.at[k], me, 1 - core).wait()
        other = sib[k].reshape(ROWS, OWN)
        mean = (total + bfdot(other, ones)) * (1.0 / MEMBERS)
        p_own = (own.astype(F32) - mean).astype(BF16)
        p_other = (other.astype(F32) - mean).astype(BF16)
        po[k] = p_own
        ps[k] = p_other
        mean_row = jnp.concatenate(
            [
                jnp.sum(jnp.where(eye, mean[c * OWN:(c + 1) * OWN], 0.0), axis=0, keepdims=True)
                for c in range(ROWS // OWN)
            ],
            axis=1,
        )

        @pl.when(k < NZ - 1)
        def _():
            pltpu.make_async_copy(vu_recv.at[k], vu_recv.at[k], vu_rsem.at[k]).wait()

        vu = vu_recv[k]
        v_row = jnp.concatenate([vu[c:c + 1] for c in range(CHUNKS)], axis=1)
        u_row = jnp.concatenate([vu[CHUNKS + c:CHUNKS + c + 1] for c in range(CHUNKS)], axis=1)
        turned = p_own.astype(F32).T
        scaled = (turned * v_row).astype(BF16)
        part_send[k, 0:OWN, 0:OWN] = bfdot(scaled, p_own).astype(BF16)
        part_send[k, 0:OWN, OWN:] = bfdot(scaled, p_other).astype(BF16)
        d_row = u_row - v_row * mean_row
        d_hi = d_row.astype(BF16).astype(F32)
        d_low = d_row - d_hi
        rows16 = lax.broadcasted_iota(jnp.int32, (16, ROWS), 0)
        d_rows = jnp.where(rows16 == 0, d_hi, jnp.where(rows16 == 1, d_low, 0.0)).astype(BF16)

        def tail(p):
            t = jnp.sum(bfdot(d_rows, p), axis=0, keepdims=True)
            hi = t.astype(BF16).astype(F32)
            rows = lax.broadcasted_iota(jnp.int32, (16, OWN), 0)
            return jnp.where(rows == 0, hi, jnp.where(rows == 1, t - hi, 0.0)).astype(BF16)

        part_send[k, OWN:, 0:OWN] = tail(p_own)
        part_send[k, OWN:, OWN:] = tail(p_other)

        @pl.when(k < NZ - 1)
        def _():
            remote(part_send.at[k], part_recv.at[k], p_ssem.at[k], p_rsem.at[k],
                   q_me * NZ + (z + depth_shift(k)) % NZ, core).start()

    total = part_send[NZ - 1].astype(F32)
    for k in range(NZ - 1):
        pltpu.make_async_copy(part_recv.at[k], part_recv.at[k], p_rsem.at[k]).wait()
        total = total + part_recv[k].astype(F32)
    mx_send[...] = total[0:OWN]
    swap = remote(mx_send, mx_recv, m_ssem, m_rsem, me, 1 - core)
    swap.start()
    innov = jnp.sum(total[OWN:], axis=0, keepdims=True)
    swap.wait()
    crossed = mx_recv[...]
    gram = jnp.concatenate(
        [total[0:OWN], jnp.concatenate([crossed[:, OWN:], crossed[:, :OWN]], axis=1)], axis=0
    )
    identity = jnp.where(
        lax.broadcasted_iota(jnp.int32, (MEMBERS, MEMBERS), 0)
        == lax.broadcasted_iota(jnp.int32, (MEMBERS, MEMBERS), 1), 1.0, 0.0,
    )
    system = (MEMBERS - 1.0) * identity + gram
    frob = jnp.sqrt(jnp.sum(jnp.sum(system * system, axis=0, keepdims=True), axis=1, keepdims=True))
    scaled = system * (1.0 / frob)
    update = 1.5 * identity - 0.5 * scaled
    inverse = halves(update)
    iterate = halves(matmul(halves(scaled), inverse))
    for sweep in range(1, ITERS):
        update = halves(1.5 * identity - 0.5 * matmul(inverse, iterate))
        if sweep < ITERS - 1:
            iterate = halves(matmul(iterate, update))
        last = matmul(update, inverse)
        inverse = halves(last)
    root = last * lax.rsqrt(frob)
    innov8 = jnp.broadcast_to(innov, (8, MEMBERS))
    mean_row = matmul(halves(matmul(halves(innov8), inverse)), inverse)[0:1] * (1.0 / frob)
    mean_col = jnp.broadcast_to(mean_row, (OWN, MEMBERS)).T
    g_recv[NZ - 1] = (
        mean_col + jnp.sqrt(MEMBERS - 1.0) * root[:, 0:OWN] - identity[:, 0:OWN]
    ).astype(BF16)

    def send_weights(k):
        remote(g_recv.at[NZ - 1], g_recv.at[k], g_ssem.at[k], g_rsem.at[k],
               q_me * NZ + (z + NZ - depth_shift(k)) % NZ, core).start()

    send_weights(NZ - 2)
    send_weights(NZ - 3)

    @pl.loop(0, NZ)
    def _(i):
        k = NZ - 1 - i

        @pl.when(k < NZ - 1)
        def _():
            pltpu.make_async_copy(g_recv.at[k], g_recv.at[k], g_rsem.at[k]).wait()

        g = g_recv[k]
        incr = bfdot(po[k], g[0:OWN]) + bfdot(ps[k], g[OWN:])
        ret_send[k] = incr.astype(BF16).reshape(NQ, CELLS, OWN)
        r = q_me * NZ + (z + depth_shift(k)) % NZ
        ret_recv[r] = ret_send[k, q_me]
        for dx, dy in SHIFTS:
            to = plane_peer(dx, dy)
            remote(ret_send.at[k, to], ret_recv.at[r], r_ssem, r_rsem, to * NZ + z, core).start()

        @pl.when(i < 2)
        def _():
            send_weights(NZ - 4 - 2 * i)
            send_weights(NZ - 5 - 2 * i)

        @pl.when(i == 2)
        def _():
            send_weights(0)

    count = NZ * (NQ - 1)
    done = ret_recv.at[pl.ds(0, count)]
    pltpu.make_async_copy(done, done, r_rsem).wait()

    @pl.loop(0, BLOCKS // GROUP)
    def _(g):
        for t in range(GROUP):
            i = g * GROUP + t
            r = dest[i]
            out[i] = (fc[r] + ret_recv[r].astype(F32)).astype(BF16)

    pltpu.make_async_copy(done, done, r_ssem).wait()

    @pl.loop(0, NZ)
    def _(k):
        block = send.at[k, pl.ds(0, NQ - 1)]
        pltpu.make_async_copy(block, block, a_send.at[k]).wait()

        @pl.when(k < NZ - 1)
        def _():
            pltpu.make_async_copy(vu_send.at[k], vu_send.at[k], vu_ssem.at[k]).wait()
            pltpu.make_async_copy(part_send.at[k], part_send.at[k], p_ssem.at[k]).wait()
            pltpu.make_async_copy(g_recv.at[k], g_recv.at[k], g_ssem.at[k]).wait()


def shards(
    ensemble, couplings, neighbours, destination, obs_index, obs_class, obs_error, obs_value
):
    smem = pl.BlockSpec(memory_space=pltpu.SMEM)
    vmem = pl.BlockSpec(memory_space=pltpu.VMEM)
    hbm = pl.BlockSpec(memory_space=pl.ANY)
    dma = pltpu.SemaphoreType.DMA
    block = (CELLS, OWN)
    posterior = pl.pallas_call(
        kernel,
        out_shape=pltpu.VMEM((BLOCKS,) + block, BF16),
        in_specs=[smem, vmem, smem, vmem, hbm, hbm, vmem, vmem, vmem, vmem],
        out_specs=vmem,
        scratch_shapes=[
            pltpu.SMEM((8, REGIONS), jnp.int32),
            pltpu.VMEM((8, REGIONS), jnp.int32),
            pltpu.VMEM((BLOCKS,) + block, F32),
            pltpu.VMEM((NEIGHB, CELLS, CELLS, BLOCKS), BF16),
            pltpu.VMEM((NEIGHB // 2, (CELLS + 1) * BLOCKS, 2 * CELLS), F32),
            pltpu.VMEM((BLOCKS, CELLS, NEIGHB * CELLS), BF16),
            pltpu.VMEM((BLOCKS + 1,) + block, BF16),
            pltpu.VMEM((WINDOW + 1,) + block, BF16),
            pltpu.VMEM((WINDOW + 1,) + block, BF16),
            pltpu.VMEM((BLOCKS + 5,) + block, BF16),
            pltpu.VMEM((2 * HALO, CELLS, NEIGHB * CELLS), BF16),
            pltpu.VMEM((8, REGIONS), jnp.int32),
            pltpu.VMEM((2, 8, REGIONS), jnp.int32),
            pltpu.SMEM((2, 8, REGIONS), jnp.int32),
            pltpu.VMEM((REGIONS,) + block, F32),
            pltpu.VMEM((NZ, NQ) + block, BF16),
            pltpu.VMEM((NZ, NQ) + block, BF16),
            pltpu.VMEM((NZ, NQ) + block, BF16),
            pltpu.VMEM((NZ, ROWS, OWN), BF16),
            pltpu.VMEM((NZ, ROWS, OWN), BF16),
            pltpu.VMEM((NZ, NQ) + block, BF16),
            pltpu.VMEM((REGIONS,) + block, BF16),
            pltpu.VMEM((NZ, 2 * CHUNKS, OWN), F32),
            pltpu.VMEM((NZ, 2 * CHUNKS, OWN), F32),
            pltpu.VMEM((NZ, PART, MEMBERS), BF16),
            pltpu.VMEM((NZ - 1, PART, MEMBERS), BF16),
            pltpu.VMEM((OWN, MEMBERS), F32),
            pltpu.VMEM((OWN, MEMBERS), F32),
            pltpu.VMEM((NZ, MEMBERS, OWN), BF16),
            dma((3,)), dma((NEIGHB,)), dma, dma, dma((6,)), dma((6,)),
            dma((NZ,)), dma((NZ,)), dma((NZ,)), dma((NZ,)),
            dma((NZ,)), dma((NZ,)), dma((NZ,)), dma((NZ,)),
            dma, dma, dma((NZ,)), dma((NZ,)), dma, dma,
        ],
        compiler_params=pltpu.CompilerParams(
            collective_id=0, has_side_effects=True, vmem_limit_bytes=58 << 20
        ),
        cost_estimate=pl.CostEstimate(
            flops=4_000_000_000, bytes_accessed=16_000_000, transcendentals=0
        ),
    )(
        neighbours.T, neighbours.T, destination, destination.reshape(1, BLOCKS), ensemble.reshape((BLOCKS,) + block),
        jnp.transpose(couplings, (1, 2, 3, 0)), obs_index, obs_class, obs_error, obs_value,
    )
    return posterior.reshape(BLOCKS * CELLS, OWN)


def solution(mesh):
    return jax.shard_map(
        shards,
        mesh=mesh,
        in_specs=(
            P("region", "member"),
            P("region", None, None, None),
            P("region", None),
            P("region"),
            P("region", None),
            P("region", None),
            P("region", None),
            P("region", None),
        ),
        out_specs=P("region", "member"),
        check_vma=False,
    )
```

time: 302 us -> 84 us (0.28); the launches traced: 298 us -> 83.9 us
  waiting for transfers between devices: 121 us -> 0 us
  Pallas kernels: 0 us -> 82.6 us
  local copies, waits for them, and re-layouts: 65.5 us -> 1.27 us
  starting transfers between devices: 48.8 us -> 0 us
  matrix products: 26.9 us -> 0 us
  other arithmetic: 16.4 us -> 0 us
  between operations: 14.5 us -> 0.01 us
  blocking collectives: 5.61 us -> 0 us
    all_to_all x2 -> x0, waiting for transfers between devices: 102 us -> none  [the longest x1 52.2 us: shards(): lax.all_to_all(incr_low.reshape(regions, slots_peer * cells_block, own_me...]
    pallas_call x0 -> x1, Pallas kernels: none -> 82.6 us  [shards(): pl.pallas_call(kernel, out_shape=pltpu.VMEM((BLOCKS,) + block, BF16), in_...]
    gather x5 -> x0, local copies, waits for them, and re-layouts: 34.7 us -> none  [the longest x2 26.6 us: shards(): picked = extended[neighbours]]
    dot_general x18 -> x0, matrix products: 26.9 us -> none  [the longest x2 16.4 us: shards(): jnp.einsum('ijcd,ijdk->ick', couplings, picked, preferred_element_type=jn...]
    all_to_all x2 -> x0, starting transfers between devices: 26.4 us -> none  [the longest x1 13.9 us: shards(): lax.all_to_all(incr_low.reshape(regions, slots_peer * cells_block, own_me...]
    ppermute x4 -> x0, starting transfers between devices: 22.3 us -> none  [the longest x2 16.6 us: padded(): lax.ppermute(head, axis, [((i + 1) % count, i) for i in range(ends)])]
    reduce_scatter x1 -> x0, waiting for transfers between devices: 17.2 us -> none  [shards(): lax.psum_scatter(partial_term, 'member', scatter_dimension=1, tiled=True)]
    scatter x1 -> x0, local copies, waits for them, and re-layouts: 15.7 us -> none  [shards(): outgoing = jnp.zeros((slot_count, cells_block, own_members), jnp.bfloat16...]
  transfers between devices with their start and end apart: 7 -> 0, of which waited for: 4 -> 0; matrix products, arithmetic and copies ran while one was open for 4% -> 0% of each run, Pallas kernels for 0% -> 0%
where the time goes in v1:
time: 84 us; the launch traced here: 83.9 us
  Pallas kernels  82.6 us (98%)
  local copies, waits for them, and re-layouts  1.27 us (2%)
    pallas_call x1, Pallas kernels, shards(): pl.pallas_call(kernel, out_shape=pltpu.VMEM((BLOCKS,) + block, BF16), in_...  82.6 us

profile of v1, /device:TPU:2, one launch (start us, length us, event | category | flops | bytes accessed | tf_op | source)
XLA Modules:
  0.0 83.9 jit_solution(3499866705963046943)
XLA Ops:
  0.0 82.6 %shard_map.82 = bf16[120,64,128]{2,1,0:T(8,128)(2,1)S(1)} custom-call(s32[4,120]{1,0:T(4,128)} %bitcast.8, s32[4,120]{1,0:T(4,128)} %bitcast.9, s32[120]{0:T(128)} %dest.1, s32[1,120]{1,0:T(1,128)} %bitcast.10, f32[120,64,128]{2,1,0:T(8,128)} %bitcast.7, bf16[4,64,64,120]{3,2,1,0:T(8,128)(2,1)} %bitcast.6, s32[1,512]{1,0:T(1,128)} %obs_index.1, ...), custom_call_target="tpu_custom_call" | custom-call | flops 4000000000 | bytes 16000000 | tf_op jit(solution)/shard_map/pallas_call | solution.py:445
  82.6 1.3 %copy.10 = bf16[7680,128]{1,0:T(8,128)(2,1)} copy(bf16[7680,128]{1,0:T(8,128)(2,1)S(1)} %bitcast.5) | data formatting | bytes 3932160

commit v2 on v1

--- a/solution.py
+++ b/solution.py
@@ -19,8 +19,10 @@
 ITERS = 4
 ROWS = NQ * CELLS
 GROUP = 8
+HALF = NZ // 2
 HALO = 2
 WINDOW = 8
+LISTS_AT = 11
 PART = OWN + 16
 CHUNKS = ROWS // OWN
 F32 = jnp.float32
@@ -31,8 +33,17 @@
 )
 
 
-def depth_shift(k):
-    return 4 + (1 - 2 * (k % 2)) * ((k + 1) // 2)
+def depth_shift(step, z):
+    i = NZ - 1 - step
+    t = i % HALF
+    far = i // HALF
+    half = z // HALF
+    p = z % HALF
+    up = p // 2
+    near_place = (p + (1 - 2 * up) * t + HALF) % HALF
+    far_place = (1 - up) * (HALF - 1 - t) + up * t
+    place = (1 - far) * (half * HALF + near_place) + far * ((1 - half) * HALF + far_place)
+    return (place - z + NZ) % NZ
 
 
 def bfdot(a, b):
@@ -45,7 +56,9 @@
 
 
 def matmul(a, b):
-    return bfdot(a[0], b[0]) + bfdot(a[0], b[1]) + bfdot(a[1], b[0])
+    return bfdot(
+        jnp.concatenate([a[0], a[0], a[1]], axis=1), jnp.concatenate([b[0], b[1], b[0]], axis=0)
+    )
 
 
 def kernel(
@@ -122,27 +135,27 @@
     cast(0, GROUP)
     ens_copies[1].wait()
     cast(BLOCKS - GROUP, GROUP)
+    for pair in range(NEIGHB // 2):
+        cpl_copies[2 * pair].wait()
+        cpl_copies[2 * pair + 1].wait()
+
+        @pl.loop(0, CELLS // GROUP)
+        def _(g):
+            for t in range(GROUP):
+                c = g * GROUP + t
+                slab = raw[pl.ds(2 * pair, 2), c].reshape(2 * CELLS, BLOCKS)
+                turned_cpl[pair, pl.ds(pl.multiple_of(c * BLOCKS, 8), BLOCKS)] = slab.T.astype(F32)
+
     pl.semaphore_wait(barrier, len(peers))
     nbr_send[...] = jnp.zeros_like(nbr_send)
     nbr_send[0:NEIGHB, 0:BLOCKS] = nbr_rows[...]
     sides = to_sides(0, own0.at[pl.ds(BLOCKS - 4, 4)], own0.at[pl.ds(0, 4)],
                      low.at[pl.ds(0, 4)], high.at[pl.ds(4, 4)])
     lists = to_sides(1, nbr_send, nbr_send, nbr_recv.at[0], nbr_recv.at[1])
-    for c in sides + lists:
+    for c in lists + sides:
         c.start()
     low[pl.ds(4, 4)] = own0[pl.ds(0, 4)]
     high[pl.ds(0, 4)] = own0[pl.ds(BLOCKS - 4, 4)]
-
-    for pair in range(NEIGHB // 2):
-        cpl_copies[2 * pair].wait()
-        cpl_copies[2 * pair + 1].wait()
-
-        @pl.loop(0, CELLS // GROUP)
-        def _(g):
-            for t in range(GROUP):
-                c = g * GROUP + t
-                slab = raw[pl.ds(2 * pair, 2), c].reshape(2 * CELLS, BLOCKS)
-                turned_cpl[pair, pl.ds(pl.multiple_of(c * BLOCKS, 8), BLOCKS)] = slab.T.astype(F32)
 
     ens_copies[2].wait()
 
@@ -172,18 +185,19 @@
         places = [jnp.clip(nbr[j, i] - HALO, 0, BLOCKS) for j in range(NEIGHB)]
         ext1[i + HALO] = route(cmat[i], own0, places).astype(BF16)
 
-    @pl.loop(0, (BLOCKS - 4) // GROUP)
-    def _(g):
+    def inner_group(g):
         for t in range(GROUP):
             inner(HALO + g * GROUP + t)
 
-    for i in range(HALO + (BLOCKS - 4) // GROUP * GROUP, BLOCKS - HALO):
-        inner(i)
-
+    pl.loop(0, LISTS_AT)(inner_group)
     for c in lists:
         c.wait()
     far_copy = pltpu.make_async_copy(nbr_recv, nbr_far, far_sem)
     far_copy.start()
+    pl.loop(LISTS_AT, (BLOCKS - 4) // GROUP)(inner_group)
+    for i in range(HALO + (BLOCKS - 4) // GROUP * GROUP, BLOCKS - HALO):
+        inner(i)
+
     for c in sides:
         c.wait()
 
@@ -228,8 +242,9 @@
     inv_copy.wait()
 
     @pl.loop(0, NZ)
-    def _(k):
-        zr = (z + depth_shift(k)) % NZ
+    def _(step):
+        k = depth_shift(step, z)
+        zr = (z + k) % NZ
         for q in range(NQ):
             r = q * NZ + zr
             b = inv[0, r]
@@ -270,12 +285,12 @@
             lanes = slice(c * OWN, (c + 1) * OWN)
             vu_send[p, c:c + 1] = v_all[p:p + 1, lanes]
             vu_send[p, CHUNKS + c:CHUNKS + c + 1] = u_all[p:p + 1, lanes]
-    vu_recv[NZ - 1] = vu_send[z]
-
-    @pl.loop(0, NZ - 1)
-    def _(k):
-        to = (z + NZ - depth_shift(k)) % NZ
-        remote(vu_send.at[to], vu_recv.at[k], vu_ssem.at[k], vu_rsem.at[k],
+    vu_recv[0] = vu_send[z]
+
+    @pl.loop(1, NZ)
+    def _(d):
+        to = (z + NZ - d) % NZ
+        remote(vu_send.at[to], vu_recv.at[d], vu_ssem.at[d], vu_rsem.at[d],
                q_me * NZ + to, core).start()
 
     ones = jnp.ones((OWN, OWN), BF16)
@@ -289,7 +304,8 @@
         remote(recv.at[k], sib.at[k], sx_send.at[k], sx_recv.at[k], me, 1 - core).start()
 
     @pl.loop(0, NZ)
-    def _(k):
+    def _(step):
+        k = depth_shift(step, z)
         start_exchange(k)
         own = recv[k].reshape(ROWS, OWN)
         total = bfdot(own, ones)
@@ -308,7 +324,7 @@
             axis=1,
         )
 
-        @pl.when(k < NZ - 1)
+        @pl.when(k > 0)
         def _():
             pltpu.make_async_copy(vu_recv.at[k], vu_recv.at[k], vu_rsem.at[k]).wait()
 
@@ -334,13 +350,13 @@
         part_send[k, OWN:, 0:OWN] = tail(p_own)
         part_send[k, OWN:, OWN:] = tail(p_other)
 
-        @pl.when(k < NZ - 1)
+        @pl.when(k > 0)
         def _():
             remote(part_send.at[k], part_recv.at[k], p_ssem.at[k], p_rsem.at[k],
-                   q_me * NZ + (z + depth_shift(k)) % NZ, core).start()
-
-    total = part_send[NZ - 1].astype(F32)
-    for k in range(NZ - 1):
+                   q_me * NZ + (z + k) % NZ, core).start()
+
+    total = part_send[0].astype(F32)
+    for k in range(1, NZ):
         pltpu.make_async_copy(part_recv.at[k], part_recv.at[k], p_rsem.at[k]).wait()
         total = total + part_recv[k].astype(F32)
     mx_send[...] = total[0:OWN]
@@ -372,42 +388,39 @@
     innov8 = jnp.broadcast_to(innov, (8, MEMBERS))
     mean_row = matmul(halves(matmul(halves(innov8), inverse)), inverse)[0:1] * (1.0 / frob)
     mean_col = jnp.broadcast_to(mean_row, (OWN, MEMBERS)).T
-    g_recv[NZ - 1] = (
+    g_recv[0] = (
         mean_col + jnp.sqrt(MEMBERS - 1.0) * root[:, 0:OWN] - identity[:, 0:OWN]
     ).astype(BF16)
 
-    def send_weights(k):
-        remote(g_recv.at[NZ - 1], g_recv.at[k], g_ssem.at[k], g_rsem.at[k],
-               q_me * NZ + (z + NZ - depth_shift(k)) % NZ, core).start()
-
-    send_weights(NZ - 2)
-    send_weights(NZ - 3)
+    def send_weights(step):
+        d = depth_shift(step, z)
+        remote(g_recv.at[0], g_recv.at[NZ - d], g_ssem.at[d], g_rsem.at[NZ - d],
+               q_me * NZ + (z + d) % NZ, core).start()
+
+    for step in range(NZ - 2, HALF - 1, -1):
+        send_weights(step)
 
     @pl.loop(0, NZ)
     def _(i):
-        k = NZ - 1 - i
-
-        @pl.when(k < NZ - 1)
+        k = depth_shift(NZ - 1 - i, z)
+
+        @pl.when(k > 0)
         def _():
             pltpu.make_async_copy(g_recv.at[k], g_recv.at[k], g_rsem.at[k]).wait()
 
         g = g_recv[k]
         incr = bfdot(po[k], g[0:OWN]) + bfdot(ps[k], g[OWN:])
         ret_send[k] = incr.astype(BF16).reshape(NQ, CELLS, OWN)
-        r = q_me * NZ + (z + depth_shift(k)) % NZ
+        r = q_me * NZ + (z + k) % NZ
         ret_recv[r] = ret_send[k, q_me]
         for dx, dy in SHIFTS:
             to = plane_peer(dx, dy)
             remote(ret_send.at[k, to], ret_recv.at[r], r_ssem, r_rsem, to * NZ + z, core).start()
 
-        @pl.when(i < 2)
+        @pl.when(i == 0)
         def _():
-            send_weights(NZ - 4 - 2 * i)
-            send_weights(NZ - 5 - 2 * i)
-
-        @pl.when(i == 2)
-        def _():
-            send_weights(0)
+            for step in range(HALF - 1, -1, -1):
+                send_weights(step)
 
     count = NZ * (NQ - 1)
     done = ret_recv.at[pl.ds(0, count)]
@@ -427,7 +440,7 @@
         block = send.at[k, pl.ds(0, NQ - 1)]
         pltpu.make_async_copy(block, block, a_send.at[k]).wait()
 
-        @pl.when(k < NZ - 1)
+        @pl.when(k > 0)
         def _():
             pltpu.make_async_copy(vu_send.at[k], vu_send.at[k], vu_ssem.at[k]).wait()
             pltpu.make_async_copy(part_send.at[k], part_send.at[k], p_ssem.at[k]).wait()
@@ -473,7 +486,7 @@
             pltpu.VMEM((NZ, 2 * CHUNKS, OWN), F32),
             pltpu.VMEM((NZ, 2 * CHUNKS, OWN), F32),
             pltpu.VMEM((NZ, PART, MEMBERS), BF16),
-            pltpu.VMEM((NZ - 1, PART, MEMBERS), BF16),
+            pltpu.VMEM((NZ, PART, MEMBERS), BF16),
             pltpu.VMEM((OWN, MEMBERS), F32),
             pltpu.VMEM((OWN, MEMBERS), F32),
             pltpu.VMEM((NZ, MEMBERS, OWN), BF16),

time: 84 us -> 85.4 us (1.017)
  no operation moved by 1% of the time
where the time goes in v2:
time: 85.4 us; the launch traced here: 84.6 us
  Pallas kernels  83.4 us (98%)
  local copies, waits for them, and re-layouts  1.27 us (1%)
    pallas_call x1, Pallas kernels, shards(): pl.pallas_call(kernel, out_shape=pltpu.VMEM((BLOCKS,) + block, BF16), in_...  83.4 us

profile of v2, /device:TPU:2, one launch (start us, length us, event | category | flops | bytes accessed | tf_op | source)
XLA Modules:
  0.0 84.6 jit_solution(15364193705771476312)
XLA Ops:
  0.0 83.4 %shard_map.82 = bf16[120,64,128]{2,1,0:T(8,128)(2,1)S(1)} custom-call(s32[4,120]{1,0:T(4,128)} %bitcast.8, s32[4,120]{1,0:T(4,128)} %bitcast.9, s32[120]{0:T(128)} %dest.1, s32[1,120]{1,0:T(1,128)} %bitcast.10, f32[120,64,128]{2,1,0:T(8,128)} %bitcast.7, bf16[4,64,64,120]{3,2,1,0:T(8,128)(2,1)} %bitcast.6, s32[1,512]{1,0:T(1,128)} %obs_index.1, ...), custom_call_target="tpu_custom_call" | custom-call | flops 4000000000 | bytes 16000000 | tf_op jit(solution)/shard_map/pallas_call | solution.py:458
  83.4 1.3 %copy.10 = bf16[7680,128]{1,0:T(8,128)(2,1)} copy(bf16[7680,128]{1,0:T(8,128)(2,1)S(1)} %bitcast.5) | data formatting | bytes 3932160

commit v3 on v2

--- a/solution.py
+++ b/solution.py
@@ -135,17 +135,6 @@
     cast(0, GROUP)
     ens_copies[1].wait()
     cast(BLOCKS - GROUP, GROUP)
-    for pair in range(NEIGHB // 2):
-        cpl_copies[2 * pair].wait()
-        cpl_copies[2 * pair + 1].wait()
-
-        @pl.loop(0, CELLS // GROUP)
-        def _(g):
-            for t in range(GROUP):
-                c = g * GROUP + t
-                slab = raw[pl.ds(2 * pair, 2), c].reshape(2 * CELLS, BLOCKS)
-                turned_cpl[pair, pl.ds(pl.multiple_of(c * BLOCKS, 8), BLOCKS)] = slab.T.astype(F32)
-
     pl.semaphore_wait(barrier, len(peers))
     nbr_send[...] = jnp.zeros_like(nbr_send)
     nbr_send[0:NEIGHB, 0:BLOCKS] = nbr_rows[...]
@@ -156,6 +145,17 @@
         c.start()
     low[pl.ds(4, 4)] = own0[pl.ds(0, 4)]
     high[pl.ds(0, 4)] = own0[pl.ds(BLOCKS - 4, 4)]
+
+    for pair in range(NEIGHB // 2):
+        cpl_copies[2 * pair].wait()
+        cpl_copies[2 * pair + 1].wait()
+
+        @pl.loop(0, CELLS // GROUP)
+        def _(g):
+            for t in range(GROUP):
+                c = g * GROUP + t
+                slab = raw[pl.ds(2 * pair, 2), c].reshape(2 * CELLS, BLOCKS)
+                turned_cpl[pair, pl.ds(pl.multiple_of(c * BLOCKS, 8), BLOCKS)] = slab.T.astype(F32)
 
     ens_copies[2].wait()
 

time: 85.4 us -> 85.7 us (level)
  no operation moved by 1% of the time
where the time goes in v3:
time: 85.7 us; the launch traced here: 85 us
  Pallas kernels  83.7 us (98%)
  local copies, waits for them, and re-layouts  1.27 us (1%)
    pallas_call x1, Pallas kernels, shards(): pl.pallas_call(kernel, out_shape=pltpu.VMEM((BLOCKS,) + block, BF16), in_...  83.7 us

profile of v3, /device:TPU:2, one launch (start us, length us, event | category | flops | bytes accessed | tf_op | source)
XLA Modules:
  0.0 85.0 jit_solution(2966902084935964695)
XLA Ops:
  0.0 83.7 %shard_map.82 = bf16[120,64,128]{2,1,0:T(8,128)(2,1)S(1)} custom-call(s32[4,120]{1,0:T(4,128)} %bitcast.8, s32[4,120]{1,0:T(4,128)} %bitcast.9, s32[120]{0:T(128)} %dest.1, s32[1,120]{1,0:T(1,128)} %bitcast.10, f32[120,64,128]{2,1,0:T(8,128)} %bitcast.7, bf16[4,64,64,120]{3,2,1,0:T(8,128)(2,1)} %bitcast.6, s32[1,512]{1,0:T(1,128)} %obs_index.1, ...), custom_call_target="tpu_custom_call" | custom-call | flops 4000000000 | bytes 16000000 | tf_op jit(solution)/shard_map/pallas_call | solution.py:458
  83.7 1.3 %copy.10 = bf16[7680,128]{1,0:T(8,128)(2,1)} copy(bf16[7680,128]{1,0:T(8,128)(2,1)S(1)} %bitcast.5) | data formatting | bytes 3932160

commit v4 on v1

--- a/solution.py
+++ b/solution.py
@@ -84,20 +84,44 @@
     cpl_copies = [
         pltpu.make_async_copy(cpl_hbm.at[j], raw.at[j], cpl_sem.at[j]) for j in range(NEIGHB)
     ]
-    for c in cpl_copies + ens_copies[2:]:
-        c.start()
-
     barrier = pltpu.get_barrier_semaphore()
     peers = [(plane_peer(dx, dy) * NZ + z, core) for dx, dy in SHIFTS]
     peers += [(q_me * NZ + (z + d) % NZ, core) for d in range(1, NZ)]
     peers += [(me, 1 - core), (right, core), (left, core)]
     for p in peers:
         pl.semaphore_signal(barrier, 1, device_id=p, device_id_type=MESH)
+    for c in cpl_copies + ens_copies[2:]:
+        c.start()
+
+    nbr_send[...] = jnp.zeros_like(nbr_send)
+    nbr_send[0:NEIGHB, 0:BLOCKS] = nbr_rows[...]
     zero_block = jnp.zeros((1, CELLS, OWN), BF16)
     own0[pl.ds(BLOCKS, 1)] = zero_block
     low[pl.ds(WINDOW, 1)] = zero_block
     high[pl.ds(WINDOW, 1)] = zero_block
     ext1[pl.ds(BLOCKS + 4, 1)] = zero_block
+
+    def cast(a, n):
+        own0[pl.ds(a, n)] = ens[pl.ds(a, n)].astype(BF16)
+
+    def to_sides(i, upper, lower, from_left, from_right):
+        return [
+            remote(upper, from_left, halo_send.at[2 * i], halo_recv.at[2 * i], right, core),
+            remote(lower, from_right, halo_send.at[2 * i + 1], halo_recv.at[2 * i + 1], left, core),
+        ]
+
+    ens_copies[0].wait()
+    cast(0, GROUP)
+    ens_copies[1].wait()
+    cast(BLOCKS - GROUP, GROUP)
+    pl.semaphore_wait(barrier, len(peers))
+    sides = to_sides(0, own0.at[pl.ds(BLOCKS - 4, 4)], own0.at[pl.ds(0, 4)],
+                     low.at[pl.ds(0, 4)], high.at[pl.ds(4, 4)])
+    lists = to_sides(1, nbr_send, nbr_send, nbr_recv.at[0], nbr_recv.at[1])
+    for c in sides + lists:
+        c.start()
+    low[pl.ds(4, 4)] = own0[pl.ds(0, 4)]
+    high[pl.ds(0, 4)] = own0[pl.ds(BLOCKS - 4, 4)]
 
     hit = lax.broadcasted_iota(jnp.int32, (REGIONS, BLOCKS), 0) == dest_row[...]
     numbers = (lax.broadcasted_iota(jnp.int32, (8, BLOCKS), 1) + 1).astype(F32).astype(BF16)
@@ -108,30 +132,6 @@
     inv_rows[...] = jnp.minimum(found, float(BLOCKS)).astype(jnp.int32) - 1
     inv_copy = pltpu.make_async_copy(inv_rows, inv, inv_sem)
     inv_copy.start()
-
-    def cast(a, n):
-        own0[pl.ds(a, n)] = ens[pl.ds(a, n)].astype(BF16)
-
-    def to_sides(i, upper, lower, from_left, from_right):
-        return [
-            remote(upper, from_left, halo_send.at[2 * i], halo_recv.at[2 * i], right, core),
-            remote(lower, from_right, halo_send.at[2 * i + 1], halo_recv.at[2 * i + 1], left, core),
-        ]
-
-    ens_copies[0].wait()
-    cast(0, GROUP)
-    ens_copies[1].wait()
-    cast(BLOCKS - GROUP, GROUP)
-    pl.semaphore_wait(barrier, len(peers))
-    nbr_send[...] = jnp.zeros_like(nbr_send)
-    nbr_send[0:NEIGHB, 0:BLOCKS] = nbr_rows[...]
-    sides = to_sides(0, own0.at[pl.ds(BLOCKS - 4, 4)], own0.at[pl.ds(0, 4)],
-                     low.at[pl.ds(0, 4)], high.at[pl.ds(4, 4)])
-    lists = to_sides(1, nbr_send, nbr_send, nbr_recv.at[0], nbr_recv.at[1])
-    for c in sides + lists:
-        c.start()
-    low[pl.ds(4, 4)] = own0[pl.ds(0, 4)]
-    high[pl.ds(0, 4)] = own0[pl.ds(BLOCKS - 4, 4)]
 
     for pair in range(NEIGHB // 2):
         cpl_copies[2 * pair].wait()

time: 84 us -> 84.2 us (level)
  no operation moved by 1% of the time
where the time goes in v4:
time: 84.2 us; the launch traced here: 84.1 us
  Pallas kernels  82.8 us (98%)
  local copies, waits for them, and re-layouts  1.27 us (2%)
    pallas_call x1, Pallas kernels, shards(): pl.pallas_call(kernel, out_shape=pltpu.VMEM((BLOCKS,) + block, BF16), in_...  82.8 us

profile of v4, /device:TPU:2, one launch (start us, length us, event | category | flops | bytes accessed | tf_op | source)
XLA Modules:
  0.0 84.1 jit_solution(11092385114485584953)
XLA Ops:
  0.0 82.8 %shard_map.82 = bf16[120,64,128]{2,1,0:T(8,128)(2,1)S(1)} custom-call(s32[4,120]{1,0:T(4,128)} %bitcast.8, s32[4,120]{1,0:T(4,128)} %bitcast.9, s32[120]{0:T(128)} %dest.1, s32[1,120]{1,0:T(1,128)} %bitcast.10, f32[120,64,128]{2,1,0:T(8,128)} %bitcast.7, bf16[4,64,64,120]{3,2,1,0:T(8,128)(2,1)} %bitcast.6, s32[1,512]{1,0:T(1,128)} %obs_index.1, ...), custom_call_target="tpu_custom_call" | custom-call | flops 4000000000 | bytes 16000000 | tf_op jit(solution)/shard_map/pallas_call | solution.py:445
  82.8 1.3 %copy.10 = bf16[7680,128]{1,0:T(8,128)(2,1)} copy(bf16[7680,128]{1,0:T(8,128)(2,1)S(1)} %bitcast.5) | data formatting | bytes 3932160
